TPU v7x, 32 devices: a whole 2x2x4 slice. The times are simulated.
32 devices in a mesh: kvh: 4 (over z), blk: 8 (over y, x, core).
Axes of the slice: x: 2, y: 2, z: 4, core: 2. Of those that a mesh axis runs over, the one named last changes fastest.
Arguments:
- queries: bfloat16 [1024, 4096], P('blk', 'kvh')
- suffix_key_rows: bfloat16 [1024, 1024], P('blk', 'kvh')
- suffix_value_rows: bfloat16 [1024, 1024], P('blk', 'kvh'), may hold values from -6 to 6
- prefix_block_keys: bfloat16 [128, 128, 1024], P('blk', None, 'kvh')
- prefix_block_values: bfloat16 [128, 128, 1024], P('blk', None, 'kvh'), may hold values from -6 to 6
- block_group: int32 [128], P('blk'), may hold values from 0 to 3, as said below
- suffix_len: int32 [16], replicated, may hold values from 32 to 96, as said below
- request_group: int32 [16], replicated, may hold values from 0 to 3, as said below
- w_out: bfloat16 [4096, 4096], P('kvh'), may hold values from -1.5 to 1.5
Outputs:
- output: bfloat16 [1024, 4096], P('blk', 'kvh')
Inputs may be any that keep to these rules, and one draw needn't show every extreme that they name: `block_group`: every group owns exactly 32 blocks; no index of blk holds more than 4 blocks of one group, and some holds exactly 4. `request_group`: every group has exactly 4 requests. `suffix_len`: the lengths sum to 1024; both ends of the range are reached; no request begins at a multiple of 128 other than 0.
All inputs are finite; a program needn't handle non-finite values.
Results may differ from a plain program's by a relative error of at most 0.005.
Values may be sent and summed in bfloat16 or wider, within the bound.
A program may use at most 256 MiB of HBM per device.

v0:
```python
import functools
import math

import jax
import jax.numpy as jnp
from jax import lax
from jax.experimental import pallas as pl
from jax.experimental.pallas import tpu as pltpu
from jax.sharding import PartitionSpec as P

HEAD_SIZE = 128
SUB = 32
MESH = pl.DeviceIdType.MESH
BF = jnp.bfloat16
F32 = jnp.float32


def dot_t(a, b):
    return lax.dot_general(a, b, (((1,), (1,)), ((), ())), preferred_element_type=F32)


def kernel(
    chips,
    depth,
    len_ref,
    group_ref,
    owner_ref,
    q_ref,
    sk_ref,
    sv_ref,
    k_hbm,
    v_hbm,
    w_hbm,
    out_ref,
    edge_tab,
    first_tab,
    last_tab,
    block_tab,
    k_ref,
    v_ref,
    w_ref,
    pk_ref,
    pv_ref,
    q_same,
    q_other,
    o_same,
    o_other,
    o_back,
    o_pair,
    o_home,
    near_o,
    l_same,
    l_work,
    l_other,
    l_back,
    l_pair,
    l_home,
    near_l,
    att_ref,
    z_out,
    z_in,
    load_sem,
    near_sem,
    q_sem,
    f_sem,
    u_sem,
    c_sem,
    z_sem,
):
    z = lax.axis_index("kvh")
    b = lax.axis_index("blk")
    chip = b // 2
    core = b % 2
    other = 1 - core
    sibling = chip * 2 + other
    blk_count = chips * 2
    tok, q_cols = q_ref.shape
    kv = sk_ref.shape[1] // HEAD_SIZE
    heads = q_cols // HEAD_SIZE
    width = heads // kv
    reqs = len_ref.shape[0]
    groups = reqs // 4
    blocks = k_ref.shape[0]
    subs = tok // SUB
    c2 = math.log2(math.e) / math.sqrt(HEAD_SIZE)

    loads = [
        pltpu.make_async_copy(k_hbm, k_ref, load_sem.at[0]),
        pltpu.make_async_copy(v_hbm, v_ref, load_sem.at[1]),
        pltpu.make_async_copy(w_hbm, w_ref, load_sem.at[2]),
    ]
    for load in loads:
        load.start()

    barrier = pltpu.get_barrier_semaphore()

    def greet(z_to, b_to):
        pl.semaphore_signal(barrier, inc=1, device_id=(z_to, b_to), device_id_type=MESH)

    greet(z, sibling)
    for k in range(1, chips):
        greet(z, lax.rem(chip + k, chips) * 2 + core)
    for d in range(1, depth):
        greet(lax.rem(z + d, depth), b)
    greet(z, lax.rem(b + blk_count - 1, blk_count))

    @pl.loop(0, groups)
    def _(g):
        per = blocks // groups
        rank = jnp.int32(0)
        found = [jnp.int32(0)] * per
        for i in range(blocks):
            hit = owner_ref[i] == g
            found = [
                jnp.where(jnp.logical_and(hit, rank == j), i, found[j]) for j in range(per)
            ]
            rank = rank + jnp.where(hit, 1, 0)
        for j in range(per):
            block_tab[g * per + j] = found[j]

    @pl.loop(0, blk_count * subs)
    def _(s):
        row = s * SUB
        start = jnp.int32(0)
        edge = first = last = jnp.int32(0)
        for r in range(reqs):
            end = start + len_ref[r]
            group = group_ref[r]
            here = start <= row
            edge = jnp.where(here, end, edge)
            first = jnp.where(here, group, first)
            last = jnp.where(start <= row + (SUB - 1), group, last)
            start = end
        edge_tab[s] = edge - row
        first_tab[s] = first
        last_tab[s] = last

    pl.semaphore_wait(barrier, chips + depth)

    def remote(src, dst, send, recv, b_to, z_to=None):
        return pltpu.make_async_remote_copy(
            src_ref=src,
            dst_ref=dst,
            send_sem=send,
            recv_sem=recv,
            device_id=(z if z_to is None else z_to, b_to),
            device_id_type=MESH,
        )

    def q_copy(k):
        return remote(
            q_ref,
            q_same.at[k],
            q_sem.at[0, k],
            q_sem.at[1, k],
            lax.rem(chip + k, chips) * 2 + core,
        )

    def f_copy(k, src):
        return remote(src, q_other.at[k], f_sem.at[0, k], f_sem.at[1, k], sibling)

    def u_copies(k):
        return (
            remote(o_other.at[k], o_back.at[k], u_sem.at[0, k], u_sem.at[1, k], sibling),
            remote(l_other.at[k], l_back.at[k], u_sem.at[2, k], u_sem.at[3, k], sibling),
        )

    def c_copies(k):
        to = lax.rem(chip + chips - k, chips) * 2 + core
        return (
            remote(o_pair.at[k], o_home.at[k], c_sem.at[0, k], c_sem.at[1, k], to),
            remote(l_pair.at[k], l_home.at[k], c_sem.at[2, k], c_sem.at[3, k], to),
        )

    f_copy(0, q_ref).start()
    for k in range(1, chips):
        q_copy(k).start()
    after = lax.rem(b + 1, blk_count)
    near_copies = (
        remote(sk_ref, pk_ref, near_sem.at[0], near_sem.at[1], after),
        remote(sv_ref, pv_ref, near_sem.at[2], near_sem.at[3], after),
    )
    for copy in near_copies:
        copy.start()
    loads[0].wait()
    loads[1].wait()

    lane = lax.broadcasted_iota(jnp.int32, (SUB, HEAD_SIZE), 1)
    sub_row = lax.broadcasted_iota(jnp.int32, (SUB, HEAD_SIZE), 0)
    per = blocks // groups

    def attend(q_in, tile, o_out, l_out):
        @pl.loop(0, subs)
        def _(i):
            s = tile * subs + i
            rows = pl.ds(pl.multiple_of(i * SUB, SUB), SUB)
            q = q_in[rows, :]
            upper = jnp.where(sub_row < edge_tab[s], 1.0, 0.0)
            upper = jnp.concatenate([upper] * width, axis=0)
            upper16 = upper.astype(BF)
            a_blocks = [block_tab[first_tab[s] * per + j] for j in range(per)]
            b_blocks = [block_tab[last_tab[s] * per + j] for j in range(per)]
            stat = jnp.zeros((SUB, HEAD_SIZE), F32)
            for g in range(kv):
                cols = slice(g * HEAD_SIZE, (g + 1) * HEAD_SIZE)
                qs = jnp.concatenate(
                    [
                        q[:, (g * width + j) * HEAD_SIZE : (g * width + j + 1) * HEAD_SIZE]
                        for j in range(width)
                    ],
                    axis=0,
                )
                qa = qs * upper16
                both = jnp.concatenate([qa, qs - qa], axis=1)
                keys = jnp.concatenate(
                    [
                        jnp.concatenate([k_ref[x][:, cols], k_ref[y][:, cols]], axis=1)
                        for x, y in zip(a_blocks, b_blocks)
                    ],
                    axis=0,
                )
                values = jnp.concatenate(
                    [
                        jnp.concatenate([v_ref[x][:, cols], v_ref[y][:, cols]], axis=1)
                        for x, y in zip(a_blocks, b_blocks)
                    ],
                    axis=0,
                )
                scores = dot_t(both, keys)
                top = jnp.max(scores, axis=1, keepdims=True) * c2
                prob = jnp.exp2(scores * c2 - top)
                total = jnp.sum(prob, axis=1, keepdims=True)
                mixed = jnp.dot(prob.astype(BF), values, preferred_element_type=F32)
                context = jnp.where(upper > 0.5, mixed[:, :HEAD_SIZE], mixed[:, HEAD_SIZE:])
                context = (context * (1.0 / total)).astype(BF)
                level = top + jnp.log2(total)
                for j in range(width):
                    h = g * width + j
                    part = slice(j * SUB, (j + 1) * SUB)
                    o_out[rows, h * HEAD_SIZE : (h + 1) * HEAD_SIZE] = context[part]
                    stat = jnp.where(lane == h, level[part], stat)
            l_out[rows, :] = stat

    def thin(stat):
        return jnp.transpose(stat)[:heads]

    def wide(flat):
        return jnp.transpose(jnp.concatenate([flat] * (HEAD_SIZE // heads), axis=0))

    def attend_other(k, q_in):
        tile = lax.rem(chip + chips - k, chips) * 2 + other
        attend(q_in, tile, o_other.at[k], l_work)
        l_other[k] = thin(l_work[...])
        for copy in u_copies(k):
            copy.start()

    def attend_same(k, q_in):
        tile = lax.rem(chip + chips - k, chips) * 2 + core
        attend(q_in, tile, o_same.at[k], l_same.at[k])

    def pair(k, o_out, l_out):
        for copy in u_copies(k):
            copy.wait_recv()
        la = l_same[k]
        lb = wide(l_back[k])
        top = jnp.maximum(la, lb)
        wa = jnp.exp2(la - top)
        wb = jnp.exp2(lb - top)
        total = wa + wb
        l_out[...] = thin(top + jnp.log2(total))
        wa = wa / total
        wb = wb / total
        for h in range(heads):
            cols = slice(h * HEAD_SIZE, (h + 1) * HEAD_SIZE)
            o_out[:, cols] = (
                o_same[k, :, cols].astype(F32) * wa[:, h : h + 1]
                + o_back[k, :, cols].astype(F32) * wb[:, h : h + 1]
            ).astype(BF)

    attend_same(0, q_ref)
    f_copy(0, q_ref).wait_recv()
    attend_other(0, q_other.at[0])

    for copy in near_copies:
        copy.wait_recv()
    own_row = b * tok + lax.broadcasted_iota(jnp.int32, (tok, 2 * tok), 0)
    key_row = (b - 1) * tok + lax.broadcasted_iota(jnp.int32, (tok, 2 * tok), 1)
    begin = jnp.zeros((tok, 2 * tok), jnp.int32)
    start = jnp.int32(0)
    for r in range(reqs):
        begin = jnp.where(own_row >= start, start, begin)
        start = start + len_ref[r]
    bias = jnp.where(
        jnp.logical_and(key_row >= begin, key_row <= own_row), 0.0, -jnp.inf
    )
    wide_lane = lax.broadcasted_iota(jnp.int32, (tok, HEAD_SIZE), 1)
    stat = jnp.zeros((tok, HEAD_SIZE), F32)
    for g in range(kv):
        cols = slice(g * HEAD_SIZE, (g + 1) * HEAD_SIZE)
        keys = jnp.concatenate([pk_ref[:, cols], sk_ref[:, cols]], axis=0)
        values = jnp.concatenate([pv_ref[:, cols], sv_ref[:, cols]], axis=0)
        for j in range(width):
            h = g * width + j
            hc = slice(h * HEAD_SIZE, (h + 1) * HEAD_SIZE)
            scores = dot_t(q_ref[:, hc], keys) * c2 + bias
            top = jnp.max(scores, axis=1, keepdims=True)
            prob = jnp.exp2(scores - top)
            total = jnp.sum(prob, axis=1, keepdims=True)
            context = jnp.dot(prob.astype(BF), values, preferred_element_type=F32)
            near_o[:, hc] = context * (1.0 / total)
            stat = jnp.where(wide_lane == h, top + jnp.log2(total), stat)
    near_l[...] = stat

    @pl.loop(1, chips)
    def _(k):
        q_copy(k).wait_recv()
        f_copy(k, q_same.at[k]).start()
        attend_same(k, q_same.at[k])

        @pl.when(k == 1)
        def _():
            pair(0, o_home.at[0], l_home.at[0])

        @pl.when(k > 1)
        def _():
            pair(k - 1, o_pair.at[k - 1], l_pair.at[k - 1])
            for copy in c_copies(k - 1):
                copy.start()

        f_copy(k, q_same.at[k]).wait_recv()
        attend_other(k, q_other.at[k])

    pair(chips - 1, o_pair.at[chips - 1], l_pair.at[chips - 1])
    for copy in c_copies(chips - 1):
        copy.start()

    for k in range(1, chips):
        for copy in c_copies(k):
            copy.wait_recv()
    levels = [wide(l_home[k]) for k in range(chips)]
    top = near_l[...]
    for level in levels:
        top = jnp.maximum(top, level)
    near_w = jnp.exp2(near_l[...] - top)
    weights = [jnp.exp2(level - top) for level in levels]
    total = near_w
    for weight in weights:
        total = total + weight
    near_w = near_w / total
    weights = [weight / total for weight in weights]
    for h in range(heads):
        cols = slice(h * HEAD_SIZE, (h + 1) * HEAD_SIZE)
        acc = near_o[:, cols] * near_w[:, h : h + 1]
        for k in range(chips):
            acc = acc + o_home[k, :, cols].astype(F32) * weights[k][:, h : h + 1]
        att_ref[:, cols] = acc.astype(BF)

    loads[2].wait()
    out_cols = out_ref.shape[1]
    step = 512 if out_cols % 512 == 0 else out_cols

    def z_copy(d):
        return remote(
            z_out.at[d], z_in.at[d], z_sem.at[0, d], z_sem.at[1, d], b, lax.rem(z + d, depth)
        )

    @pl.loop(1, depth)
    def _(d):
        to = lax.rem(z + d, depth)

        @pl.loop(0, out_cols // step)
        def _(t):
            at = pl.ds(pl.multiple_of(to * out_cols + t * step, step), step)
            z_out[d, :, pl.ds(pl.multiple_of(t * step, step), step)] = jnp.dot(
                att_ref[...], w_ref[:, at], preferred_element_type=F32
            ).astype(BF)

        z_copy(d).start()

    @pl.loop(0, out_cols // step)
    def _(t):
        at = pl.ds(pl.multiple_of(z * out_cols + t * step, step), step)
        near_o[:, pl.ds(pl.multiple_of(t * step, step), step)] = jnp.dot(
            att_ref[...], w_ref[:, at], preferred_element_type=F32
        )

    for d in range(1, depth):
        z_copy(d).wait_recv()
    acc = near_o[...]
    for d in range(1, depth):
        acc = acc + z_in[d].astype(F32)
    out_ref[...] = acc.astype(BF)

    for copy in near_copies:
        copy.wait_send()
    f_copy(0, q_ref).wait_send()
    for copy in u_copies(0):
        copy.wait_send()
    for k in range(1, chips):
        q_copy(k).wait_send()
        f_copy(k, q_same.at[k]).wait_send()
        for copy in u_copies(k):
            copy.wait_send()
        for copy in c_copies(k):
            copy.wait_send()
    for d in range(1, depth):
        z_copy(d).wait_send()


def per_device(
    queries,
    suffix_key_rows,
    suffix_value_rows,
    prefix_block_keys,
    prefix_block_values,
    block_group,
    suffix_len,
    request_group,
    w_out,
):
    tok, q_cols = queries.shape
    kv_cols = suffix_key_rows.shape[1]
    heads = q_cols // HEAD_SIZE
    blk_count = lax.axis_size("blk")
    depth = lax.axis_size("kvh")
    chips = blk_count // 2
    blocks = prefix_block_keys.shape[0]
    out_cols = w_out.shape[1] // depth
    subs = blk_count * tok // SUB
    smem = pl.BlockSpec(memory_space=pltpu.SMEM)
    vmem = pl.BlockSpec(memory_space=pltpu.VMEM)
    hbm = pl.BlockSpec(memory_space=pl.ANY)
    tiles = pltpu.VMEM((chips, tok, q_cols), BF)
    thin = pltpu.VMEM((chips, heads, tok), F32)
    dma = pltpu.SemaphoreType.DMA
    return pl.pallas_call(
        functools.partial(kernel, chips, depth),
        out_shape=jax.ShapeDtypeStruct((tok, out_cols), BF),
        in_specs=[smem] * 3 + [vmem] * 3 + [hbm] * 3,
        out_specs=vmem,
        scratch_shapes=[
            pltpu.SMEM((subs,), jnp.int32),
            pltpu.SMEM((subs,), jnp.int32),
            pltpu.SMEM((subs,), jnp.int32),
            pltpu.SMEM((blocks,), jnp.int32),
            pltpu.VMEM(prefix_block_keys.shape, BF),
            pltpu.VMEM(prefix_block_values.shape, BF),
            pltpu.VMEM(w_out.shape, BF),
            pltpu.VMEM((tok, kv_cols), BF),
            pltpu.VMEM((tok, kv_cols), BF),
            tiles,
            tiles,
            tiles,
            tiles,
            tiles,
            tiles,
            tiles,
            pltpu.VMEM((tok, q_cols), F32),
            pltpu.VMEM((chips, tok, HEAD_SIZE), F32),
            pltpu.VMEM((tok, HEAD_SIZE), F32),
            thin,
            thin,
            thin,
            thin,
            pltpu.VMEM((tok, HEAD_SIZE), F32),
            pltpu.VMEM((tok, q_cols), BF),
            pltpu.VMEM((depth, tok, out_cols), BF),
            pltpu.VMEM((depth, tok, out_cols), BF),
            dma((3,)),
            dma((4,)),
            dma((2, chips)),
            dma((2, chips)),
            dma((4, chips)),
            dma((4, chips)),
            dma((2, depth)),
        ],
        compiler_params=pltpu.CompilerParams(
            collective_id=0, has_side_effects=True, vmem_limit_bytes=56 * 1024 * 1024
        ),
    )(
        suffix_len,
        request_group,
        block_group,
        queries,
        suffix_key_rows,
        suffix_value_rows,
        prefix_block_keys,
        prefix_block_values,
        w_out,
    )


def solution(mesh):
    placed = (
        P("blk", "kvh"),
        P("blk", "kvh"),
        P("blk", "kvh"),
        P("blk", None, "kvh"),
        P("blk", None, "kvh"),
        P("blk"),
        P(),
        P(),
        P("kvh", None),
    )
    return jax.shard_map(
        per_device, mesh=mesh, in_specs=placed, out_specs=P("blk", "kvh"), check_vma=False
    )
```

profile of v0, /device:TPU:11, one launch (start us, length us, event | category | flops | bytes accessed | tf_op | source)
XLA Modules:
  0.0 79.0 jit_solution(15737905825471790386)
XLA Ops:
  0.0 77.3 %shard_map.91 = bf16[128,1024]{1,0:T(8,128)(2,1)} custom-call(s32[16]{0:T(128)} %len_ref.1, s32[16]{0:T(128)} %group_ref.1, s32[16]{0:T(128)} %owner_ref.1, bf16[128,1024]{1,0:T(8,128)(2,1)} %q_ref.1, bf16[128,256]{1,0:T(8,128)(2,1)} %sk_ref.1, bf16[128,256]{1,0:T(8,128)(2,1)} %sv_ref.1, bf16[16,128,256]{2,1,0:T(8,128)(2,1)} %k_hbm.1, ...), custom_call_target="tpu_custom_call" | custom-call | tf_op jit(solution)/shard_map/pallas_call | solution.py:436
  77.3 1.7 %copy.11 = bf16[128,1024]{1,0:T(8,128)(2,1)} copy(bf16[128,1024]{1,0:T(8,128)(2,1)} %shard_map.91) | data formatting | bytes 524288
where the time goes:
time: 79.2 us; the launch traced here: 79 us
  Pallas kernels  77.3 us (98%)
  local copies, waits for them, and re-layouts  1.67 us (2%)
    pallas_call x1, Pallas kernels, per_device(): pl.pallas_call(functools.partial(kernel, chips, depth), out_shape=jax.Sha...  77.3 us
    unnamed x1, local copies, waits for them, and re-layouts  1.67 us

commit v1 on v0

--- a/solution.py
+++ b/solution.py
@@ -10,6 +10,7 @@
 
 HEAD_SIZE = 128
 SUB = 32
+CHUNKS = 2
 MESH = pl.DeviceIdType.MESH
 BF = jnp.bfloat16
 F32 = jnp.float32
@@ -82,6 +83,8 @@
     groups = reqs // 4
     blocks = k_ref.shape[0]
     subs = tok // SUB
+    part_subs = subs // CHUNKS
+    size = tok // CHUNKS
     c2 = math.log2(math.e) / math.sqrt(HEAD_SIZE)
 
     loads = [
@@ -147,41 +150,64 @@
             device_id_type=MESH,
         )
 
-    def q_copy(k):
+    def span(c):
+        return pl.ds(c * size, size)
+
+    def q_copy(k, c):
         return remote(
-            q_ref,
-            q_same.at[k],
-            q_sem.at[0, k],
-            q_sem.at[1, k],
+            q_ref.at[span(c)],
+            q_same.at[k, span(c)],
+            q_sem.at[0, k, c],
+            q_sem.at[1, k, c],
             lax.rem(chip + k, chips) * 2 + core,
         )
 
-    def f_copy(k, src):
-        return remote(src, q_other.at[k], f_sem.at[0, k], f_sem.at[1, k], sibling)
-
-    def u_copies(k):
+    def f_copy(k, c, src):
+        return remote(
+            src.at[span(c)],
+            q_other.at[k, span(c)],
+            f_sem.at[0, k, c],
+            f_sem.at[1, k, c],
+            sibling,
+        )
+
+    def u_copies(k, c):
         return (
-            remote(o_other.at[k], o_back.at[k], u_sem.at[0, k], u_sem.at[1, k], sibling),
-            remote(l_other.at[k], l_back.at[k], u_sem.at[2, k], u_sem.at[3, k], sibling),
-        )
-
-    def c_copies(k):
+            remote(
+                o_other.at[k, span(c)],
+                o_back.at[k, span(c)],
+                u_sem.at[0, k, c],
+                u_sem.at[1, k, c],
+                sibling,
+            ),
+            remote(l_other.at[k, c], l_back.at[k, c], u_sem.at[2, k, c], u_sem.at[3, k, c], sibling),
+        )
+
+    def c_copies(k, c):
         to = lax.rem(chip + chips - k, chips) * 2 + core
         return (
-            remote(o_pair.at[k], o_home.at[k], c_sem.at[0, k], c_sem.at[1, k], to),
-            remote(l_pair.at[k], l_home.at[k], c_sem.at[2, k], c_sem.at[3, k], to),
-        )
-
-    f_copy(0, q_ref).start()
-    for k in range(1, chips):
-        q_copy(k).start()
+            remote(
+                o_pair.at[k, span(c)],
+                o_home.at[k, span(c)],
+                c_sem.at[0, k, c],
+                c_sem.at[1, k, c],
+                to,
+            ),
+            remote(l_pair.at[k, c], l_home.at[k, c], c_sem.at[2, k, c], c_sem.at[3, k, c], to),
+        )
+
     after = lax.rem(b + 1, blk_count)
     near_copies = (
         remote(sk_ref, pk_ref, near_sem.at[0], near_sem.at[1], after),
         remote(sv_ref, pv_ref, near_sem.at[2], near_sem.at[3], after),
     )
-    for copy in near_copies:
-        copy.start()
+    for c in range(CHUNKS):
+        f_copy(0, c, q_ref).start()
+        for k in range(1, chips):
+            q_copy(k, c).start()
+        if c == 0:
+            for copy in near_copies:
+                copy.start()
     loads[0].wait()
     loads[1].wait()
 
@@ -189,8 +215,8 @@
     sub_row = lax.broadcasted_iota(jnp.int32, (SUB, HEAD_SIZE), 0)
     per = blocks // groups
 
-    def attend(q_in, tile, o_out, l_out):
-        @pl.loop(0, subs)
+    def attend(q_in, tile, o_out, l_out, c):
+        @pl.loop(c * part_subs, (c + 1) * part_subs, unroll=part_subs)
         def _(i):
             s = tile * subs + i
             rows = pl.ds(pl.multiple_of(i * SUB, SUB), SUB)
@@ -242,27 +268,27 @@
             l_out[rows, :] = stat
 
     def thin(stat):
-        return jnp.transpose(stat)[:heads]
+        return jnp.transpose(jnp.concatenate([stat] * CHUNKS, axis=0))[:heads]
 
     def wide(flat):
-        return jnp.transpose(jnp.concatenate([flat] * (HEAD_SIZE // heads), axis=0))
-
-    def attend_other(k, q_in):
+        return jnp.transpose(jnp.concatenate([flat] * (HEAD_SIZE // heads), axis=0))[:size]
+
+    def attend_other(k, q_in, c):
         tile = lax.rem(chip + chips - k, chips) * 2 + other
-        attend(q_in, tile, o_other.at[k], l_work)
-        l_other[k] = thin(l_work[...])
-        for copy in u_copies(k):
+        attend(q_in, tile, o_other.at[k], l_work, c)
+        l_other[k, c] = thin(l_work[span(c), :])
+        for copy in u_copies(k, c):
             copy.start()
 
-    def attend_same(k, q_in):
+    def attend_same(k, q_in, c):
         tile = lax.rem(chip + chips - k, chips) * 2 + core
-        attend(q_in, tile, o_same.at[k], l_same.at[k])
-
-    def pair(k, o_out, l_out):
-        for copy in u_copies(k):
+        attend(q_in, tile, o_same.at[k], l_same.at[k], c)
+
+    def pair(k, o_out, l_out, c):
+        for copy in u_copies(k, c):
             copy.wait_recv()
-        la = l_same[k]
-        lb = wide(l_back[k])
+        la = l_same[k, span(c), :]
+        lb = wide(l_back[k, c])
         top = jnp.maximum(la, lb)
         wa = jnp.exp2(la - top)
         wb = jnp.exp2(lb - top)
@@ -272,14 +298,17 @@
         wb = wb / total
         for h in range(heads):
             cols = slice(h * HEAD_SIZE, (h + 1) * HEAD_SIZE)
-            o_out[:, cols] = (
-                o_same[k, :, cols].astype(F32) * wa[:, h : h + 1]
-                + o_back[k, :, cols].astype(F32) * wb[:, h : h + 1]
+            o_out[span(c), cols] = (
+                o_same[k, span(c), cols].astype(F32) * wa[:, h : h + 1]
+                + o_back[k, span(c), cols].astype(F32) * wb[:, h : h + 1]
             ).astype(BF)
 
-    attend_same(0, q_ref)
-    f_copy(0, q_ref).wait_recv()
-    attend_other(0, q_other.at[0])
+    def own_chip(c):
+        attend_same(0, q_ref, c)
+        f_copy(0, c, q_ref).wait_recv()
+        attend_other(0, q_other.at[0], c)
+
+    own_chip(0)
 
     for copy in near_copies:
         copy.wait_recv()
@@ -311,71 +340,82 @@
             stat = jnp.where(wide_lane == h, top + jnp.log2(total), stat)
     near_l[...] = stat
 
-    @pl.loop(1, chips)
-    def _(k):
-        q_copy(k).wait_recv()
-        f_copy(k, q_same.at[k]).start()
-        attend_same(k, q_same.at[k])
-
-        @pl.when(k == 1)
-        def _():
-            pair(0, o_home.at[0], l_home.at[0])
-
-        @pl.when(k > 1)
-        def _():
-            pair(k - 1, o_pair.at[k - 1], l_pair.at[k - 1])
-            for copy in c_copies(k - 1):
-                copy.start()
-
-        f_copy(k, q_same.at[k]).wait_recv()
-        attend_other(k, q_other.at[k])
-
-    pair(chips - 1, o_pair.at[chips - 1], l_pair.at[chips - 1])
-    for copy in c_copies(chips - 1):
-        copy.start()
-
-    for k in range(1, chips):
-        for copy in c_copies(k):
-            copy.wait_recv()
-    levels = [wide(l_home[k]) for k in range(chips)]
-    top = near_l[...]
-    for level in levels:
-        top = jnp.maximum(top, level)
-    near_w = jnp.exp2(near_l[...] - top)
-    weights = [jnp.exp2(level - top) for level in levels]
-    total = near_w
-    for weight in weights:
-        total = total + weight
-    near_w = near_w / total
-    weights = [weight / total for weight in weights]
-    for h in range(heads):
-        cols = slice(h * HEAD_SIZE, (h + 1) * HEAD_SIZE)
-        acc = near_o[:, cols] * near_w[:, h : h + 1]
-        for k in range(chips):
-            acc = acc + o_home[k, :, cols].astype(F32) * weights[k][:, h : h + 1]
-        att_ref[:, cols] = acc.astype(BF)
+    for c in range(CHUNKS):
+        if c > 0:
+            own_chip(c)
+
+        @pl.loop(1, chips)
+        def _(k):
+            q_copy(k, c).wait_recv()
+            f_copy(k, c, q_same.at[k]).start()
+            attend_same(k, q_same.at[k], c)
+
+            @pl.when(k == 1)
+            def _():
+                pair(0, o_home.at[0], l_home.at[0, c], c)
+
+            @pl.when(k > 1)
+            def _():
+                pair(k - 1, o_pair.at[k - 1], l_pair.at[k - 1, c], c)
+                for copy in c_copies(k - 1, c):
+                    copy.start()
+
+            f_copy(k, c, q_same.at[k]).wait_recv()
+            attend_other(k, q_other.at[k], c)
+
+        pair(chips - 1, o_pair.at[chips - 1], l_pair.at[chips - 1, c], c)
+        for copy in c_copies(chips - 1, c):
+            copy.start()
 
     loads[2].wait()
     out_cols = out_ref.shape[1]
     step = 512 if out_cols % 512 == 0 else out_cols
 
-    def z_copy(d):
+    def z_copy(d, c):
         return remote(
-            z_out.at[d], z_in.at[d], z_sem.at[0, d], z_sem.at[1, d], b, lax.rem(z + d, depth)
-        )
-
-    @pl.loop(1, depth)
-    def _(d):
-        to = lax.rem(z + d, depth)
-
-        @pl.loop(0, out_cols // step)
-        def _(t):
-            at = pl.ds(pl.multiple_of(to * out_cols + t * step, step), step)
-            z_out[d, :, pl.ds(pl.multiple_of(t * step, step), step)] = jnp.dot(
-                att_ref[...], w_ref[:, at], preferred_element_type=F32
-            ).astype(BF)
-
-        z_copy(d).start()
+            z_out.at[d, span(c)],
+            z_in.at[d, span(c)],
+            z_sem.at[0, d, c],
+            z_sem.at[1, d, c],
+            b,
+            lax.rem(z + d, depth),
+        )
+
+    for c in range(CHUNKS):
+        for k in range(1, chips):
+            for copy in c_copies(k, c):
+                copy.wait_recv()
+        levels = [wide(l_home[k, c]) for k in range(chips)]
+        near_level = near_l[span(c), :]
+        top = near_level
+        for level in levels:
+            top = jnp.maximum(top, level)
+        near_w = jnp.exp2(near_level - top)
+        weights = [jnp.exp2(level - top) for level in levels]
+        total = near_w
+        for weight in weights:
+            total = total + weight
+        near_w = near_w / total
+        weights = [weight / total for weight in weights]
+        for h in range(heads):
+            cols = slice(h * HEAD_SIZE, (h + 1) * HEAD_SIZE)
+            acc = near_o[span(c), cols] * near_w[:, h : h + 1]
+            for k in range(chips):
+                acc = acc + o_home[k, span(c), cols].astype(F32) * weights[k][:, h : h + 1]
+            att_ref[span(c), cols] = acc.astype(BF)
+
+        @pl.loop(1, depth)
+        def _(d):
+            to = lax.rem(z + d, depth)
+
+            @pl.loop(0, out_cols // step)
+            def _(t):
+                at = pl.ds(pl.multiple_of(to * out_cols + t * step, step), step)
+                z_out[d, span(c), pl.ds(pl.multiple_of(t * step, step), step)] = jnp.dot(
+                    att_ref[span(c), :], w_ref[:, at], preferred_element_type=F32
+                ).astype(BF)
+
+            z_copy(d, c).start()
 
     @pl.loop(0, out_cols // step)
     def _(t):
@@ -384,27 +424,29 @@
             att_ref[...], w_ref[:, at], preferred_element_type=F32
         )
 
-    for d in range(1, depth):
-        z_copy(d).wait_recv()
-    acc = near_o[...]
-    for d in range(1, depth):
-        acc = acc + z_in[d].astype(F32)
-    out_ref[...] = acc.astype(BF)
+    for c in range(CHUNKS):
+        for d in range(1, depth):
+            z_copy(d, c).wait_recv()
+        acc = near_o[span(c), :]
+        for d in range(1, depth):
+            acc = acc + z_in[d, span(c), :].astype(F32)
+        out_ref[span(c), :] = acc.astype(BF)
 
     for copy in near_copies:
         copy.wait_send()
-    f_copy(0, q_ref).wait_send()
-    for copy in u_copies(0):
-        copy.wait_send()
-    for k in range(1, chips):
-        q_copy(k).wait_send()
-        f_copy(k, q_same.at[k]).wait_send()
-        for copy in u_copies(k):
+    for c in range(CHUNKS):
+        f_copy(0, c, q_ref).wait_send()
+        for copy in u_copies(0, c):
             copy.wait_send()
-        for copy in c_copies(k):
-            copy.wait_send()
-    for d in range(1, depth):
-        z_copy(d).wait_send()
+        for k in range(1, chips):
+            q_copy(k, c).wait_send()
+            f_copy(k, c, q_same.at[k]).wait_send()
+            for copy in u_copies(k, c):
+                copy.wait_send()
+            for copy in c_copies(k, c):
+                copy.wait_send()
+        for d in range(1, depth):
+            z_copy(d, c).wait_send()
 
 
 def per_device(
@@ -431,7 +473,7 @@
     vmem = pl.BlockSpec(memory_space=pltpu.VMEM)
     hbm = pl.BlockSpec(memory_space=pl.ANY)
     tiles = pltpu.VMEM((chips, tok, q_cols), BF)
-    thin = pltpu.VMEM((chips, heads, tok), F32)
+    thin = pltpu.VMEM((chips, CHUNKS, heads, tok), F32)
     dma = pltpu.SemaphoreType.DMA
     return pl.pallas_call(
         functools.partial(kernel, chips, depth),
@@ -468,11 +510,11 @@
             pltpu.VMEM((depth, tok, out_cols), BF),
             dma((3,)),
             dma((4,)),
-            dma((2, chips)),
-            dma((2, chips)),
-            dma((4, chips)),
-            dma((4, chips)),
-            dma((2, depth)),
+            dma((2, chips, CHUNKS)),
+            dma((2, chips, CHUNKS)),
+            dma((4, chips, CHUNKS)),
+            dma((4, chips, CHUNKS)),
+            dma((2, depth, CHUNKS)),
         ],
         compiler_params=pltpu.CompilerParams(
             collective_id=0, has_side_effects=True, vmem_limit_bytes=56 * 1024 * 1024

time: 79.2 us -> 70.2 us (0.89)
  the two profiles are of different devices: /device:TPU:11 before, /device:TPU:0 now
where the time goes in v1:
time: 70.2 us; the launch traced here: 70.1 us
  Pallas kernels  68.4 us (97%)
  local copies, waits for them, and re-layouts  1.67 us (2%)
    pallas_call x1, Pallas kernels, per_device(): pl.pallas_call(functools.partial(kernel, chips, depth), out_shape=jax.Sha...  68.4 us
    unnamed x1, local copies, waits for them, and re-layouts  1.67 us

profile of v1, /device:TPU:0, one launch (start us, length us, event | category | flops | bytes accessed | tf_op | source)
XLA Modules:
  0.0 70.1 jit_solution(3357271752681737636)
XLA Ops:
  0.0 68.4 %shard_map.91 = bf16[128,1024]{1,0:T(8,128)(2,1)} custom-call(s32[16]{0:T(128)} %len_ref.1, s32[16]{0:T(128)} %group_ref.1, s32[16]{0:T(128)} %owner_ref.1, bf16[128,1024]{1,0:T(8,128)(2,1)} %q_ref.1, bf16[128,256]{1,0:T(8,128)(2,1)} %sk_ref.1, bf16[128,256]{1,0:T(8,128)(2,1)} %sv_ref.1, bf16[16,128,256]{2,1,0:T(8,128)(2,1)} %k_hbm.1, ...), custom_call_target="tpu_custom_call" | custom-call | tf_op jit(solution)/shard_map/pallas_call | solution.py:478
  68.4 1.7 %copy.11 = bf16[128,1024]{1,0:T(8,128)(2,1)} copy(bf16[128,1024]{1,0:T(8,128)(2,1)} %shard_map.91) | data formatting | bytes 524288

commit v2 on v1

--- a/solution.py
+++ b/solution.py
@@ -340,33 +340,6 @@
             stat = jnp.where(wide_lane == h, top + jnp.log2(total), stat)
     near_l[...] = stat
 
-    for c in range(CHUNKS):
-        if c > 0:
-            own_chip(c)
-
-        @pl.loop(1, chips)
-        def _(k):
-            q_copy(k, c).wait_recv()
-            f_copy(k, c, q_same.at[k]).start()
-            attend_same(k, q_same.at[k], c)
-
-            @pl.when(k == 1)
-            def _():
-                pair(0, o_home.at[0], l_home.at[0, c], c)
-
-            @pl.when(k > 1)
-            def _():
-                pair(k - 1, o_pair.at[k - 1], l_pair.at[k - 1, c], c)
-                for copy in c_copies(k - 1, c):
-                    copy.start()
-
-            f_copy(k, c, q_same.at[k]).wait_recv()
-            attend_other(k, q_other.at[k], c)
-
-        pair(chips - 1, o_pair.at[chips - 1], l_pair.at[chips - 1, c], c)
-        for copy in c_copies(chips - 1, c):
-            copy.start()
-
     loads[2].wait()
     out_cols = out_ref.shape[1]
     step = 512 if out_cols % 512 == 0 else out_cols
@@ -381,7 +354,7 @@
             lax.rem(z + d, depth),
         )
 
-    for c in range(CHUNKS):
+    def finish(c):
         for k in range(1, chips):
             for copy in c_copies(k, c):
                 copy.wait_recv()
@@ -416,6 +389,38 @@
                 ).astype(BF)
 
             z_copy(d, c).start()
+
+    for c in range(CHUNKS):
+        if c > 0:
+            own_chip(c)
+
+        @pl.loop(1, chips)
+        def _(k):
+            if c > 0:
+                pl.when(k == chips // 2)(lambda: finish(c - 1))
+
+            q_copy(k, c).wait_recv()
+            f_copy(k, c, q_same.at[k]).start()
+            attend_same(k, q_same.at[k], c)
+
+            @pl.when(k == 1)
+            def _():
+                pair(0, o_home.at[0], l_home.at[0, c], c)
+
+            @pl.when(k > 1)
+            def _():
+                pair(k - 1, o_pair.at[k - 1], l_pair.at[k - 1, c], c)
+                for copy in c_copies(k - 1, c):
+                    copy.start()
+
+            f_copy(k, c, q_same.at[k]).wait_recv()
+            attend_other(k, q_other.at[k], c)
+
+        pair(chips - 1, o_pair.at[chips - 1], l_pair.at[chips - 1, c], c)
+        for copy in c_copies(chips - 1, c):
+            copy.start()
+
+    finish(CHUNKS - 1)
 
     @pl.loop(0, out_cols // step)
     def _(t):

time: 70.2 us -> 65.9 us (0.939)
  Pallas kernels: 68.4 us -> 64.1 us
    pallas_call x1, Pallas kernels: 68.4 us -> 64.1 us  [per_device(): pl.pallas_call(functools.partial(kernel, chips, depth), out_shape=jax.Sha...]
where the time goes in v2:
time: 65.9 us; the launch traced here: 65.8 us
  Pallas kernels  64.1 us (97%)
  local copies, waits for them, and re-layouts  1.67 us (3%)
    pallas_call x1, Pallas kernels, per_device(): pl.pallas_call(functools.partial(kernel, chips, depth), out_shape=jax.Sha...  64.1 us
    unnamed x1, local copies, waits for them, and re-layouts  1.67 us

profile of v2, /device:TPU:0, one launch (start us, length us, event | category | flops | bytes accessed | tf_op | source)
XLA Modules:
  0.0 65.8 jit_solution(4977126352890763575)
XLA Ops:
  0.0 64.1 %shard_map.91 = bf16[128,1024]{1,0:T(8,128)(2,1)} custom-call(s32[16]{0:T(128)} %len_ref.1, s32[16]{0:T(128)} %group_ref.1, s32[16]{0:T(128)} %owner_ref.1, bf16[128,1024]{1,0:T(8,128)(2,1)} %q_ref.1, bf16[128,256]{1,0:T(8,128)(2,1)} %sk_ref.1, bf16[128,256]{1,0:T(8,128)(2,1)} %sv_ref.1, bf16[16,128,256]{2,1,0:T(8,128)(2,1)} %k_hbm.1, ...), custom_call_target="tpu_custom_call" | custom-call | tf_op jit(solution)/shard_map/pallas_call | solution.py:483
  64.1 1.7 %copy.11 = bf16[128,1024]{1,0:T(8,128)(2,1)} copy(bf16[128,1024]{1,0:T(8,128)(2,1)} %shard_map.91) | data formatting | bytes 524288

commit v3 on v2

--- a/solution.py
+++ b/solution.py
@@ -308,37 +308,39 @@
         f_copy(0, c, q_ref).wait_recv()
         attend_other(0, q_other.at[0], c)
 
+    def near():
+        for copy in near_copies:
+            copy.wait_recv()
+        own_row = b * tok + lax.broadcasted_iota(jnp.int32, (tok, 2 * tok), 0)
+        key_row = (b - 1) * tok + lax.broadcasted_iota(jnp.int32, (tok, 2 * tok), 1)
+        begin = jnp.zeros((tok, 2 * tok), jnp.int32)
+        start = jnp.int32(0)
+        for r in range(reqs):
+            begin = jnp.where(own_row >= start, start, begin)
+            start = start + len_ref[r]
+        bias = jnp.where(
+            jnp.logical_and(key_row >= begin, key_row <= own_row), 0.0, -jnp.inf
+        )
+        wide_lane = lax.broadcasted_iota(jnp.int32, (tok, HEAD_SIZE), 1)
+        stat = jnp.zeros((tok, HEAD_SIZE), F32)
+        for g in range(kv):
+            cols = slice(g * HEAD_SIZE, (g + 1) * HEAD_SIZE)
+            keys = jnp.concatenate([pk_ref[:, cols], sk_ref[:, cols]], axis=0)
+            values = jnp.concatenate([pv_ref[:, cols], sv_ref[:, cols]], axis=0)
+            for j in range(width):
+                h = g * width + j
+                hc = slice(h * HEAD_SIZE, (h + 1) * HEAD_SIZE)
+                scores = dot_t(q_ref[:, hc], keys) * c2 + bias
+                top = jnp.max(scores, axis=1, keepdims=True)
+                prob = jnp.exp2(scores - top)
+                total = jnp.sum(prob, axis=1, keepdims=True)
+                context = jnp.dot(prob.astype(BF), values, preferred_element_type=F32)
+                near_o[:, hc] = context * (1.0 / total)
+                stat = jnp.where(wide_lane == h, top + jnp.log2(total), stat)
+        near_l[...] = stat
+
     own_chip(0)
 
-    for copy in near_copies:
-        copy.wait_recv()
-    own_row = b * tok + lax.broadcasted_iota(jnp.int32, (tok, 2 * tok), 0)
-    key_row = (b - 1) * tok + lax.broadcasted_iota(jnp.int32, (tok, 2 * tok), 1)
-    begin = jnp.zeros((tok, 2 * tok), jnp.int32)
-    start = jnp.int32(0)
-    for r in range(reqs):
-        begin = jnp.where(own_row >= start, start, begin)
-        start = start + len_ref[r]
-    bias = jnp.where(
-        jnp.logical_and(key_row >= begin, key_row <= own_row), 0.0, -jnp.inf
-    )
-    wide_lane = lax.broadcasted_iota(jnp.int32, (tok, HEAD_SIZE), 1)
-    stat = jnp.zeros((tok, HEAD_SIZE), F32)
-    for g in range(kv):
-        cols = slice(g * HEAD_SIZE, (g + 1) * HEAD_SIZE)
-        keys = jnp.concatenate([pk_ref[:, cols], sk_ref[:, cols]], axis=0)
-        values = jnp.concatenate([pv_ref[:, cols], sv_ref[:, cols]], axis=0)
-        for j in range(width):
-            h = g * width + j
-            hc = slice(h * HEAD_SIZE, (h + 1) * HEAD_SIZE)
-            scores = dot_t(q_ref[:, hc], keys) * c2 + bias
-            top = jnp.max(scores, axis=1, keepdims=True)
-            prob = jnp.exp2(scores - top)
-            total = jnp.sum(prob, axis=1, keepdims=True)
-            context = jnp.dot(prob.astype(BF), values, preferred_element_type=F32)
-            near_o[:, hc] = context * (1.0 / total)
-            stat = jnp.where(wide_lane == h, top + jnp.log2(total), stat)
-    near_l[...] = stat
 
     loads[2].wait()
     out_cols = out_ref.shape[1]
@@ -393,6 +395,8 @@
     for c in range(CHUNKS):
         if c > 0:
             own_chip(c)
+        if c == 1:
+            near()
 
         @pl.loop(1, chips)
         def _(k):

time: 65.9 us -> 61.9 us (0.939)
  Pallas kernels: 64.1 us -> 60 us
    pallas_call x1, Pallas kernels: 64.1 us -> 60 us  [per_device(): pl.pallas_call(functools.partial(kernel, chips, depth), out_shape=jax.Sha...]
where the time goes in v3:
time: 61.9 us; the launch traced here: 61.7 us
  Pallas kernels  60 us (97%)
  local copies, waits for them, and re-layouts  1.67 us (3%)
    pallas_call x1, Pallas kernels, per_device(): pl.pallas_call(functools.partial(kernel, chips, depth), out_shape=jax.Sha...  60 us
    unnamed x1, local copies, waits for them, and re-layouts  1.67 us

profile of v3, /device:TPU:0, one launch (start us, length us, event | category | flops | bytes accessed | tf_op | source)
XLA Modules:
  0.0 61.7 jit_solution(3085927230362673250)
XLA Ops:
  0.0 60.0 %shard_map.91 = bf16[128,1024]{1,0:T(8,128)(2,1)} custom-call(s32[16]{0:T(128)} %len_ref.1, s32[16]{0:T(128)} %group_ref.1, s32[16]{0:T(128)} %owner_ref.1, bf16[128,1024]{1,0:T(8,128)(2,1)} %q_ref.1, bf16[128,256]{1,0:T(8,128)(2,1)} %sk_ref.1, bf16[128,256]{1,0:T(8,128)(2,1)} %sv_ref.1, bf16[16,128,256]{2,1,0:T(8,128)(2,1)} %k_hbm.1, ...), custom_call_target="tpu_custom_call" | custom-call | tf_op jit(solution)/shard_map/pallas_call | solution.py:487
  60.0 1.7 %copy.11 = bf16[128,1024]{1,0:T(8,128)(2,1)} copy(bf16[128,1024]{1,0:T(8,128)(2,1)} %shard_map.91) | data formatting | bytes 524288
